TPU v7x, 512 devices: a whole 4x8x8 slice. The times are simulated.
512 devices in a mesh: section: 16 (over y, core), blk: 32 (over x, z).
Axes of the slice: x: 4, y: 8, z: 8, core: 2. Of those that a mesh axis runs over, the one named last changes fastest.
Arguments:
- residual: float32 [24576, 32, 128], P(('section', 'blk')), may hold values from -6 to 6
- kin_inverse: float32 [24576, 32, 32], P(('section', 'blk'))
- cell_weight: float32 [24576, 128], P(('section', 'blk')), may hold values from 0.5 to 1
- upwind_frac: float32 [24576, 4, 128], P(('section', 'blk')), may hold values from 0.2 to 0.7
- block_level: int32 [24576], P(('section', 'blk')), may hold values from 0 to 5, as said below
- send_in: int32 [512, 5, 32], P(('section', 'blk')), may hold values from 0 to 48, as said below
- send_down: int32 [512, 5, 32], P(('section', 'blk')), may hold values from 0 to 48, as said below
- upwind_slot: int32 [24576, 4], P(('section', 'blk')), may hold values from 0 to 368, as said below
Outputs:
- newton_step: float32 [24576, 32, 128], P(('section', 'blk'))
Inputs may be any that keep to these rules, and one draw needn't show every extreme that they name: `block_level`: on each device the blocks of levels 0 to 5 number 48 * 8 / 24, 6 / 24, 4 / 24, 3 / 24, 2 / 24 and 1 / 24 in some cyclic order of the levels, so one level holds 16 blocks of every device. `send_in`: an entry other than 48 names a block of level l on the sending device, for entry [d, l, i]. About half of the entries are none; for every section and level some device receives a block from every device of its section. `send_down`: as send_in, for the owner i of the next section. The last section sends none; for every other section and level some device of the next section receives a block from every device of the sending section. `upwind_slot`: every source of a block has a lower level than the block (a slot of send level l counts as level l), and a slot that is named holds a block; blocks of level 0 have none.
All inputs are finite; a program needn't handle non-finite values.
Results may differ from a plain program's by a relative error of at most 0.0001.
Values sent between devices are 32-bit elements; how exact they have to be, the bound alone decides.
A program may use at most 64 MiB of HBM per device.

v0:
```python
import functools

import jax
import jax.numpy as jnp
from jax import lax
from jax.experimental import pallas as pl
from jax.experimental.pallas import tpu as pltpu
from jax.sharding import PartitionSpec as P

LEVELS = 6
ROUNDS = 5
CAP = 16
BLOCKS = 48
UPW = 4
PEERS = 32
ZERO = LEVELS * CAP
ARRIVED = ZERO + 1
STORE = ARRIVED + 2 * ROUNDS * PEERS
T_BLOCK, T_REF = 0, 96
T_SEND = T_REF + 96 * UPW
T_SLOT = T_SEND + 2 * ROUNDS * PEERS
T_LEN = T_SLOT + BLOCKS
MESH = pl.DeviceIdType.MESH


def solve_level(level, tab, residual, kin, weight, frac, store):
    def one(k, _):
        place = level * CAP + k
        b = tab[T_BLOCK + place]
        inflow = residual[b]
        fractions = frac[b]
        for j in range(UPW):
            source = store[tab[T_REF + place * UPW + j]]
            inflow = inflow + fractions[j : j + 1, :] * source
        mixed = jnp.dot(
            kin[b], inflow, precision=lax.Precision.HIGHEST, preferred_element_type=jnp.float32
        )
        store[place] = weight[b] * mixed
        return 0

    lax.fori_loop(0, CAP, one, 0, unroll=4)


def kernel(
    sections, tab, residual, kin, weight, frac, out, store, sendb, arrived, send_sem, recv_sem
):
    sec = lax.axis_index("section")
    me = lax.axis_index("blk")
    has_next = sec < sections - 1
    has_prev = sec > 0
    barrier = pltpu.get_barrier_semaphore()

    def greet(o, _):
        peer = lax.rem(me + o, PEERS)

        @pl.when(o > 0)
        def _():
            pl.semaphore_signal(
                barrier, inc=1, device_id={"section": sec, "blk": peer}, device_id_type=MESH
            )

        @pl.when(has_prev)
        def _():
            pl.semaphore_signal(
                barrier, inc=1, device_id={"section": sec - 1, "blk": peer}, device_id_type=MESH
            )

        return 0

    lax.fori_loop(0, PEERS, greet, 0)
    store[ZERO] = jnp.zeros(store.shape[1:], jnp.float32)
    solve_level(0, tab, residual, kin, weight, frac, store)

    @pl.when(has_next)
    def _():
        pl.semaphore_wait(barrier, 2 * PEERS - 1)

    @pl.when(jnp.logical_not(has_next))
    def _():
        pl.semaphore_wait(barrier, PEERS - 1)

    def copy_to(way, level, peer, section):
        return pltpu.make_async_remote_copy(
            src_ref=sendb.at[way, level, peer],
            dst_ref=arrived.at[way, level, me],
            send_sem=send_sem.at[way, level],
            recv_sem=recv_sem.at[way, level],
            device_id={"section": section, "blk": peer},
            device_id_type=MESH,
        )

    def one_round(level, _):
        def send(o, _):
            peer = lax.rem(me + o, PEERS)
            sendb[0, level, peer] = store[tab[T_SEND + level * PEERS + peer]]

            @pl.when(o > 0)
            def _():
                copy_to(0, level, peer, sec).start()

            @pl.when(has_next)
            def _():
                sendb[1, level, peer] = store[tab[T_SEND + (ROUNDS + level) * PEERS + peer]]
                copy_to(1, level, peer, sec + 1).start()

            return 0

        lax.fori_loop(0, PEERS, send, 0)

        some = arrived.at[0, level, pl.ds(0, PEERS - 1)]
        pltpu.make_async_copy(some, some, recv_sem.at[0, level]).wait()

        def keep_in(i, _):
            store[ARRIVED + level * PEERS + i] = arrived[0, level, i]
            return 0

        own = sendb[0, level, me]
        lax.fori_loop(0, PEERS, keep_in, 0, unroll=8)
        store[ARRIVED + level * PEERS + me] = own

        base = ARRIVED + (ROUNDS + level) * PEERS

        @pl.when(has_prev)
        def _():
            every = arrived.at[1, level]
            pltpu.make_async_copy(every, every, recv_sem.at[1, level]).wait()

            def keep_down(i, _):
                store[base + i] = arrived[1, level, i]
                return 0

            lax.fori_loop(0, PEERS, keep_down, 0, unroll=8)

        @pl.when(jnp.logical_not(has_prev))
        def _():
            def blank(i, _):
                store[base + i] = jnp.zeros(store.shape[1:], jnp.float32)
                return 0

            lax.fori_loop(0, PEERS, blank, 0, unroll=8)

        solve_level(level + 1, tab, residual, kin, weight, frac, store)
        return 0

    lax.fori_loop(0, ROUNDS, one_round, 0)

    def give(b, _):
        out[b] = store[tab[T_SLOT + b]]
        return 0

    lax.fori_loop(0, BLOCKS, give, 0, unroll=8)

    def finish(level, _):
        some = sendb.at[0, level, pl.ds(0, PEERS - 1)]
        pltpu.make_async_copy(some, some, send_sem.at[0, level]).wait()

        @pl.when(has_next)
        def _():
            every = sendb.at[1, level]
            pltpu.make_async_copy(every, every, send_sem.at[1, level]).wait()

        return 0

    lax.fori_loop(0, ROUNDS, finish, 0)


def tables(block_level, send_in, send_down, upwind_slot):
    ids = jnp.arange(BLOCKS, dtype=jnp.int32)
    places = jnp.arange(LEVELS * CAP, dtype=jnp.int32)
    same = (block_level[:, None] == block_level[None, :]) & (ids[None, :] < ids[:, None])
    slot = block_level * CAP + jnp.sum(same.astype(jnp.int32), axis=1)

    def slot_of(local):
        hit = local[..., None] == ids
        return ZERO + jnp.sum(jnp.where(hit, slot - ZERO, 0), axis=-1)

    sends = slot_of(jnp.concatenate([send_in.reshape(-1), send_down.reshape(-1)]))
    refs = jnp.where(
        upwind_slot <= BLOCKS, slot_of(upwind_slot), upwind_slot - (BLOCKS + 1) + ARRIVED
    )
    at = slot[None, :] == places[:, None]
    block_at = jnp.sum(jnp.where(at, ids, 0), axis=1)
    refs_at = ZERO + jnp.sum(jnp.where(at[:, :, None], refs[None] - ZERO, 0), axis=1)
    return jnp.concatenate([block_at, refs_at.reshape(-1), sends, slot])


def shards(
    residual, kin_inverse, cell_weight, upwind_frac, block_level, send_in, send_down, upwind_slot
):
    blocks, species, cells = residual.shape
    tab = tables(block_level, send_in, send_down, upwind_slot)
    vmem = pl.BlockSpec(memory_space=pltpu.VMEM)
    return pl.pallas_call(
        functools.partial(kernel, lax.axis_size("section")),
        out_shape=jax.ShapeDtypeStruct(residual.shape, jnp.float32),
        in_specs=[pl.BlockSpec(memory_space=pltpu.SMEM)] + [vmem] * 4,
        out_specs=vmem,
        scratch_shapes=[
            pltpu.VMEM((STORE, species, cells), jnp.float32),
            pltpu.VMEM((2, ROUNDS, PEERS, species, cells), jnp.float32),
            pltpu.VMEM((2, ROUNDS, PEERS, species, cells), jnp.float32),
            pltpu.SemaphoreType.DMA((2, ROUNDS)),
            pltpu.SemaphoreType.DMA((2, ROUNDS)),
        ],
        compiler_params=pltpu.CompilerParams(
            collective_id=0, has_side_effects=True, vmem_limit_bytes=40 * 1024 * 1024
        ),
    )(tab, residual, kin_inverse, cell_weight[:, None, :], upwind_frac)


def solution(mesh):
    both = ("section", "blk")
    return jax.shard_map(
        shards,
        mesh=mesh,
        in_specs=(
            P(both, None, None),
            P(both, None, None),
            P(both, None),
            P(both, None, None),
            P(both),
            P(both, None, None),
            P(both, None, None),
            P(both, None),
        ),
        out_specs=P(both, None, None),
        check_vma=False,
    )
```

profile of v0, /device:TPU:11, one launch (start us, length us, event | category | flops | bytes accessed | tf_op | source)
XLA Modules:
  0.0 166.8 jit_solution(4930570131713133867)
XLA Ops:
  0.0 0.0 copy-start.3
  0.0 0.0 copy-start
  0.0 0.7 copy-done.3
  0.7 0.2 convert_reduce_fusion
  0.8 0.1 select_reduce_fusion.3
  0.9 0.9 select_reduce_fusion.1
  1.8 0.7 select_add_fusion
  2.5 0.7 reduce
  3.2 0.1 reshape.33
  3.3 0.7 reduce.1
  4.0 0.1 reshape.34
  4.1 0.1 pad_add_fusion.1
  4.2 0.1 select_reduce_fusion.2
  4.3 0.1 iota_compare_fusion.2
  4.4 0.1 select_reduce_fusion
  4.5 0.1 copy.15
  4.6 0.1 add.41
  4.7 0.1 pad_add_fusion.tab
  4.8 0.0 copy-start.1
  4.8 0.0 copy-start.2
  4.8 1.8 %copy.16.kin = f32[48,32,32]{2,1,0:T(8,128)S(1)} copy(f32[48,32,32]{0,2,1:T(8,128)} %param.9) | data formatting | bytes 393216 | tf_op args[1]
  6.6 0.0 copy-done
  6.6 0.0 copy-done.1
  6.6 0.0 copy-done.2
  6.6 159.3 %shard_map.82 = f32[48,32,128]{2,1,0:T(8,128)S(1)} custom-call(s32[848]{0:T(1024)S(1)} %pad_add_fusion.tab, f32[48,32,128]{2,1,0:T(8,128)S(1)} %copy-done, f32[48,32,32]{2,1,0:T(8,128)S(1)} %copy.16.kin, f32[48,1,128]{2,1,0:T(1,128)S(1)} %bitcast.1, f32[48,4,128]{2,1,0:T(4,128)S(1)} %copy-done.1), custom_call_target="tpu_custom_call" | custom-call | tf_op jit(solution)/shard_map/pallas_call | solution.py:193
  165.9 0.9 copy.18
  (3 shorter events, 0.0 us)
Async XLA Ops:
  0.0 0.7 copy-start.3
  0.0 6.6 %copy-start = (f32[48,32,128]{2,1,0:T(8,128)S(1)}, f32[48,32,128]{2,1,0:T(8,128)}, u32[]{:S(2)}) copy-start(f32[48,32,128]{2,1,0:T(8,128)} %residual.1) | copy-start | bytes 2359300
  4.8 1.8 %copy-start.1 = (f32[48,4,128]{2,1,0:T(4,128)S(1)}, f32[48,4,128]{2,1,0:T(4,128)}, u32[]{:S(2)}) copy-start(f32[48,4,128]{2,1,0:T(4,128)} %frac.1) | copy-start | bytes 294916
  4.8 1.8 %copy-start.2 = (f32[48,128]{1,0:T(8,128)S(1)}, f32[48,128]{1,0:T(8,128)}, u32[]{:S(2)}) copy-start(f32[48,128]{1,0:T(8,128)} %param.10) | copy-start | bytes 73732
where the time goes:
time: 167 us
  Pallas kernels  159 us (95%)
  other arithmetic  3.72 us (2%)
  local copies, waits for them, and re-layouts  3.69 us (2%)
    pallas_call x1, Pallas kernels, shards(): pl.pallas_call(functools.partial(kernel, lax.axis_size('section')), out_s...  159 us

commit v1 on v0

v1 whole, which is shorter than its diff:
```python
import functools

import jax
import jax.numpy as jnp
from jax import lax
from jax.experimental import pallas as pl
from jax.experimental.pallas import tpu as pltpu
from jax.sharding import PartitionSpec as P

LEVELS = 6
ROUNDS = 5
CAP = 16
BLOCKS = 48
GROUP = 8
UPW = 4
ZS, XS = 8, 4
PEERS = XS * ZS
NEAR = 5
ZERO = LEVELS * CAP
ARRIVED = ZERO + 1
STORE = ARRIVED + 2 * ROUNDS * PEERS
T_BLOCK, T_REF, T_SLOT, T_SEND, T_ROWS = 0, 1, 5, 8, 24
E_ROW1 = 2 * XS * NEAR
E_ROW2 = E_ROW1 + 4 * XS
ENTRIES = E_ROW2 + 2 * XS
MESH = pl.DeviceIdType.MESH
ROWS = 16
HALF = 64


def swap(value):
    return pltpu.roll(value, HALF, 1)


def low_lanes(rows):
    return lax.broadcasted_iota(jnp.int32, (rows, 2 * HALF), 1) < HALF


def fold(half, top, bottom):
    low = low_lanes(top.shape[0])
    return (
        jnp.where(low, top, swap(bottom)) if half == 0 else jnp.where(low, swap(top), bottom)
    )


def make_table(z, level_ref, upwind_ref, send_in_ref, send_down_ref, table):
    square = (BLOCKS, BLOCKS)
    wide = (BLOCKS, 2 * HALF)
    row, col = (lax.broadcasted_iota(jnp.int32, square, d) for d in range(2))

    def down(mask, value):
        return jnp.sum(jnp.where(mask, value, 0), axis=0, keepdims=True)

    def upright(value):
        return jnp.sum(
            jnp.where(row == col, jnp.broadcast_to(value, square), 0), axis=1, keepdims=True
        )

    level = level_ref[...]
    level_col = upright(level)
    same = jnp.broadcast_to(level, square) == level_col
    rank_col = jnp.sum(jnp.where(same & (col < row), 1, 0), axis=1, keepdims=True)
    slot_col = level_col * CAP + rank_col
    table[...] = jnp.zeros(table.shape, jnp.int32)
    table[T_SLOT : T_SLOT + 1, :BLOCKS] = down(row == col, slot_col)
    here = slot_col == lax.broadcasted_iota(jnp.int32, wide, 1)
    table[T_BLOCK : T_BLOCK + 1, :] = down(here, lax.broadcasted_iota(jnp.int32, wide, 0))
    for j in range(UPW):
        t = upwind_ref[j : j + 1, :]
        local = ZERO + down(t == row, slot_col - ZERO)
        number = jnp.maximum(t - (BLOCKS + 1), 0)
        owner_z = number & (ZS - 1)
        remote = ARRIVED + number - owner_z + ((owner_z - z + (2 + ZS)) & (ZS - 1))
        ref = jnp.where(t <= BLOCKS, local, remote)
        table[T_REF + j : T_REF + j + 1, :] = ZERO + down(here, upright(ref) - ZERO)
    local_id = lax.broadcasted_iota(jnp.int32, (BLOCKS, PEERS), 0)
    for way, sent in enumerate((send_in_ref, send_down_ref)):
        for r in range(ROUNDS):
            place = T_SEND + way * ROUNDS + r
            table[place : place + 1, :PEERS] = CAP + down(sent[r] == local_id, rank_col - CAP)


def kernel(
    sections,
    level_ref,
    upwind_ref,
    send_in_ref,
    send_down_ref,
    residual,
    kin,
    weight,
    frac,
    out,
    table,
    around,
    tab,
    tabs,
    store,
    near,
    packs,
    arrived,
    sendb,
    pack_send,
    pack_recv,
    uni_send,
    uni_recv,
    tab_send,
    tab_recv,
    tab_local,
):
    sec = lax.axis_index("section")
    me = lax.axis_index("blk")
    x, z = me // ZS, lax.rem(me, ZS)
    has_next = sec < sections - 1
    has_prev = sec > 0
    barrier = pltpu.get_barrier_semaphore()
    zeros = jnp.zeros((ROWS, 2 * HALF), jnp.float32)

    def at(section, xo, zo):
        peer = lax.rem(x + xo, XS) * ZS + lax.rem(z + zo + ZS, ZS)
        return {"section": section, "blk": peer}

    def greet(xo, _):
        for zo in range(-2, 3):
            if zo == 0:

                @pl.when(xo > 0)
                def _():
                    pl.semaphore_signal(
                        barrier, inc=1, device_id=at(sec, xo, 0), device_id_type=MESH
                    )
            else:
                pl.semaphore_signal(
                    barrier, inc=1, device_id=at(sec, xo, zo), device_id_type=MESH
                )

            @pl.when(has_prev)
            def _(zo=zo):
                pl.semaphore_signal(
                    barrier, inc=1, device_id=at(sec - 1, xo, zo), device_id_type=MESH
                )

        return 0

    lax.fori_loop(0, XS, greet, 0)

    def solve(half, level, last=False):
        low = low_lanes(ROWS)

        def gather(k):
            place = level * CAP + k
            b = tab[T_BLOCK, place]
            whole = residual[b]
            inflow = fold(half, whole[:ROWS], whole[ROWS:])
            fractions = fold(half, frac[b], frac[b])
            for j in range(UPW):
                source = store[half, tab[T_REF + j, place]]
                inflow = inflow + fractions[j : j + 1, :] * source
            other = swap(inflow)
            both = jnp.concatenate(
                [jnp.where(low, inflow, other), jnp.where(low, other, inflow)], axis=0
            )
            coarse = both.astype(jnp.bfloat16)
            rest = (both - coarse.astype(jnp.float32)).astype(jnp.bfloat16)
            return b, jnp.concatenate([coarse, coarse, rest], axis=0)

        def group(g, _):
            spots = [g * GROUP + i for i in range(GROUP)]
            gathered = [gather(k) for k in spots]
            mixed = [
                jnp.dot(kin[b], terms, preferred_element_type=jnp.float32)
                for b, terms in gathered
            ]
            solved = [
                fold(half, weight[b], weight[b]) * jnp.where(low, m[:ROWS], m[ROWS:])
                for (b, _), m in zip(gathered, mixed)
            ]
            for k, value in zip(spots, solved):
                store[half, level * CAP + k] = value
                if not last:
                    packs[half, level, 2 * CAP + k] = value
            return 0

        lax.fori_loop(0, CAP // GROUP, group, 0)

    def pack_copy(half, level, source, target, zo):
        return pltpu.make_async_remote_copy(
            src_ref=packs.at[half, level, pl.ds(source * CAP, CAP)],
            dst_ref=packs.at[half, level, pl.ds(target * CAP, CAP)],
            send_sem=pack_send.at[half, level],
            recv_sem=pack_recv.at[half, level, target],
            device_id=at(sec, 0, zo),
            device_id_type=MESH,
        )

    def pack_wait(half, level, place):
        some = packs.at[half, level, pl.ds(place * CAP, CAP)]
        pltpu.make_async_copy(some, some, pack_recv.at[half, level, place]).wait()

    def send_own(half, level):
        pack_copy(half, level, 2, 1, 1).start()
        pack_copy(half, level, 2, 3, -1).start()

    def forward(half, level):
        pack_wait(half, level, 1)
        pack_copy(half, level, 1, 0, 1).start()
        pack_wait(half, level, 3)
        pack_copy(half, level, 3, 4, -1).start()

    def deliver(half, level):
        pack_wait(half, level, 0)
        pack_wait(half, level, 4)
        for p in range(NEAR):
            for k in range(CAP):
                near[p * (CAP + 1) + k] = packs[half, level, p * CAP + k]

        def to_column(xo, _):
            column = lax.rem(x + xo, XS) * ZS

            def fill(entry, way, p, zo):
                target = column + lax.rem(z + zo + ZS, ZS)
                chosen = tabs[p, way * ROUNDS + level, target]
                sendb[half, level, entry] = near[p * (CAP + 1) + chosen]

            def copy(entry, count, way, place, zo):
                return pltpu.make_async_remote_copy(
                    src_ref=sendb.at[half, level, pl.ds(entry, count)],
                    dst_ref=arrived.at[way, half, level, pl.ds(x * ZS + place, count)],
                    send_sem=uni_send.at[way, half, level],
                    recv_sem=uni_recv.at[way, half, level],
                    device_id=at(sec + way, xo, zo),
                    device_id_type=MESH,
                )

            def send_way(way):
                far = E_ROW2 + way * XS + xo
                if way == 0:
                    fill(far, way, 0, 2)
                    copy(far, 1, way, 6, 2).start()
                else:
                    fill(far, way, 4, -2)
                    copy(far, 1, way, 6, -2).start()
                up = E_ROW1 + way * XS + xo
                fill(up, way, 0, 1)
                copy(up, 1, way, 7, 1).start()
                down = E_ROW1 + (2 + way) * XS + xo
                fill(down, way, 4, -1)
                copy(down, 1, way, 5, -1).start()
                first = (way * XS + xo) * NEAR
                for p in range(NEAR):
                    fill(first + p, way, p, 0)
                if way == 0:

                    @pl.when(xo > 0)
                    def _():
                        copy(first, NEAR, way, 0, 0).start()
                else:
                    copy(first, NEAR, way, 0, 0).start()

            send_way(0)

            @pl.when(has_next)
            def _():
                send_way(1)

            return 0

        lax.fori_loop(0, XS, to_column, 0)

    def absorb(half, level):
        some = arrived.at[0, half, level, pl.ds(0, PEERS - NEAR)]
        pltpu.make_async_copy(some, some, uni_recv.at[0, half, level]).wait()
        base = ARRIVED + level * PEERS
        for i in range(PEERS):
            store[half, base + i] = arrived[0, half, level, i]
        for p in range(NEAR):
            store[half, base + x * ZS + p] = sendb[half, level, p]

        @pl.when(has_prev)
        def _():
            every = arrived.at[1, half, level]
            pltpu.make_async_copy(every, every, uni_recv.at[1, half, level]).wait()
            for i in range(PEERS):
                store[half, base + ROUNDS * PEERS + i] = arrived[1, half, level, i]

    for half in range(2):
        store[half, ZERO] = zeros
    for p in range(NEAR):
        near[p * (CAP + 1) + CAP] = zeros

    @pl.when(jnp.logical_not(has_prev))
    def _():
        def blank(i, _):
            for half in range(2):
                store[half, ARRIVED + ROUNDS * PEERS + i] = zeros
            return 0

        lax.fori_loop(0, ROUNDS * PEERS, blank, 0)

    make_table(z, level_ref, upwind_ref, send_in_ref, send_down_ref, table)
    own = pltpu.make_async_copy(table, tab, tab_local.at[NEAR])
    own.start()
    own.wait()
    solve(0, 0)

    @pl.when(has_next)
    def _():
        pl.semaphore_wait(barrier, 2 * XS * NEAR - 1)

    @pl.when(jnp.logical_not(has_next))
    def _():
        pl.semaphore_wait(barrier, XS * NEAR - 1)

    send_own(0, 0)
    for o in (-2, -1, 1, 2):
        pltpu.make_async_remote_copy(
            src_ref=table.at[pl.ds(T_SEND, 16)],
            dst_ref=around.at[2 - o],
            send_sem=tab_send,
            recv_sem=tab_recv.at[2 - o],
            device_id=at(sec, 0, o),
            device_id_type=MESH,
        ).start()
    solve(1, 0)
    send_own(1, 0)
    moves = []
    for p in range(NEAR):
        if p == 2:
            source = table.at[pl.ds(T_SEND, 16)]
        else:
            source = around.at[p]
            pltpu.make_async_copy(source, source, tab_recv.at[p]).wait()
        moves.append(pltpu.make_async_copy(source, tabs.at[p], tab_local.at[p]))
        moves[-1].start()
    for move in moves:
        move.wait()

    def one_round(level, _):
        forward(0, level)

        @pl.when(level > 0)
        def _():
            absorb(1, level - 1)
            solve(1, level)
            send_own(1, level)

        deliver(0, level)
        forward(1, level)
        absorb(0, level)

        @pl.when(level < ROUNDS - 1)
        def _():
            solve(0, level + 1)
            send_own(0, level + 1)

        deliver(1, level)
        return 0

    lax.fori_loop(0, ROUNDS, one_round, 0)
    solve(0, ROUNDS, last=True)
    absorb(1, ROUNDS - 1)
    solve(1, ROUNDS, last=True)

    def give(b, _):
        slot = tab[T_SLOT, b]
        first, second = store[0, slot], store[1, slot]
        low = low_lanes(ROWS)
        out[b, :ROWS] = jnp.where(low, first, swap(second))
        out[b, ROWS:] = jnp.where(low, swap(first), second)
        return 0

    lax.fori_loop(0, BLOCKS, give, 0, unroll=4)

    def finish(level, _):
        for half in range(2):
            some = packs.at[half, level, pl.ds(0, 4 * CAP)]
            pltpu.make_async_copy(some, some, pack_send.at[half, level]).wait()
            some = sendb.at[half, level, pl.ds(0, PEERS - NEAR)]
            pltpu.make_async_copy(some, some, uni_send.at[0, half, level]).wait()

            @pl.when(has_next)
            def _(half=half):
                some = sendb.at[half, level, pl.ds(0, PEERS)]
                pltpu.make_async_copy(some, some, uni_send.at[1, half, level]).wait()

        return 0

    lax.fori_loop(0, ROUNDS, finish, 0)
    some = around.at[pl.ds(0, NEAR - 1)]
    pltpu.make_async_copy(some, some, tab_send).wait()


def shards(
    residual, kin_inverse, cell_weight, upwind_frac, block_level, send_in, send_down, upwind_slot
):
    blocks, species, cells = residual.shape
    coarse = lax.reduce_precision(kin_inverse, 8, 7)
    rest = (kin_inverse - coarse).astype(jnp.bfloat16)
    coarse = coarse.astype(jnp.bfloat16)
    kin = jnp.concatenate([coarse, rest, coarse], axis=2)
    vmem = pl.BlockSpec(memory_space=pltpu.VMEM)
    half = (ROWS, 2 * HALF)
    return pl.pallas_call(
        functools.partial(kernel, lax.axis_size("section")),
        out_shape=jax.ShapeDtypeStruct(residual.shape, jnp.float32),
        in_specs=[vmem] * 8,
        out_specs=vmem,
        scratch_shapes=[
            pltpu.VMEM((T_ROWS, 2 * HALF), jnp.int32),
            pltpu.VMEM((NEAR, 16, 2 * HALF), jnp.int32),
            pltpu.SMEM((T_ROWS, 2 * HALF), jnp.int32),
            pltpu.SMEM((NEAR, 16, 2 * HALF), jnp.int32),
            pltpu.VMEM((2, STORE, *half), jnp.float32),
            pltpu.VMEM((NEAR * (CAP + 1), *half), jnp.float32),
            pltpu.VMEM((2, ROUNDS, NEAR * CAP, *half), jnp.float32),
            pltpu.VMEM((2, 2, ROUNDS, PEERS, *half), jnp.float32),
            pltpu.VMEM((2, ROUNDS, ENTRIES, *half), jnp.float32),
            pltpu.SemaphoreType.DMA((2, ROUNDS)),
            pltpu.SemaphoreType.DMA((2, ROUNDS, NEAR)),
            pltpu.SemaphoreType.DMA((2, 2, ROUNDS)),
            pltpu.SemaphoreType.DMA((2, 2, ROUNDS)),
            pltpu.SemaphoreType.DMA,
            pltpu.SemaphoreType.DMA((NEAR,)),
            pltpu.SemaphoreType.DMA((NEAR + 1,)),
        ],
        compiler_params=pltpu.CompilerParams(
            collective_id=0, has_side_effects=True, vmem_limit_bytes=44 * 1024 * 1024
        ),
    )(
        block_level[None],
        upwind_slot.T,
        send_in.transpose(1, 0, 2),
        send_down.transpose(1, 0, 2),
        residual,
        kin,
        cell_weight[:, None, :],
        upwind_frac,
    )


def solution(mesh):
    both = ("section", "blk")
    return jax.shard_map(
        shards,
        mesh=mesh,
        in_specs=(
            P(both, None, None),
            P(both, None, None),
            P(both, None),
            P(both, None, None),
            P(both),
            P(both, None, None),
            P(both, None, None),
            P(both, None),
        ),
        out_specs=P(both, None, None),
        check_vma=False,
    )
```

time: 167 us -> 131 us (0.78)
  the two profiles are of different devices: /device:TPU:11 before, /device:TPU:41 now
where the time goes in v1:
time: 131 us; the launch traced here: 130 us
  Pallas kernels  125 us (95%)
  local copies, waits for them, and re-layouts  3.33 us (3%)
  other arithmetic  1.61 us (1%)
    pallas_call x1, Pallas kernels, shards(): pl.pallas_call(functools.partial(kernel, lax.axis_size('section')), out_s...  125 us
    unnamed x18, local copies, waits for them, and re-layouts  2.63 us

profile of v1, /device:TPU:41, one launch (start us, length us, event | category | flops | bytes accessed | tf_op | source)
XLA Modules:
  0.0 130.3 jit_solution(8385935994924412038)
XLA Ops:
  0.0 1.1 reduce_precision.3
  1.1 0.0 copy-start.7
  1.1 0.7 copy.11
  1.8 0.3 copy-done.7
  2.1 0.7 copy.12
  2.8 0.2 subtract_convert_fusion
  3.0 0.0 copy-start
  3.0 0.0 copy-start.1
  3.0 0.0 copy-start.2
  3.0 0.0 copy-start.3
  3.1 0.0 copy-start.4
  3.1 0.0 copy-start.5
  3.1 0.0 copy-start.6
  3.1 0.4 pad_maximum_fusion.kin
  3.5 0.7 copy-done
  4.1 0.0 copy-done.1
  4.1 0.0 copy-done.2
  4.1 0.0 copy-done.3
  4.2 0.0 copy-done.4
  4.2 0.0 copy-done.5
  4.2 0.0 copy-done.6
  4.2 125.2 %shard_map.82 = f32[48,32,128]{2,1,0:T(8,128)S(1)} custom-call(s32[1,48]{1,0:T(1,128)S(1)} %bitcast.9, s32[4,48]{1,0:T(4,128)S(1)} %bitcast.8, s32[5,1,32]{2,1,0:T(1,128)S(1)} %bitcast.6, s32[5,1,32]{2,1,0:T(1,128)S(1)} %bitcast.7, f32[48,32,128]{2,1,0:T(8,128)S(1)} %copy-done, bf16[48,32,96]{2,1,0:T(8,128)(2,1)S(1)} %pad_maximum_fusion.kin, ...), custom_call_target="tpu_custom_call" | custom-call | tf_op jit(solution)/shard_map/pallas_call | solution.py:403
  129.4 0.9 copy.15
Async XLA Ops:
  1.1 1.0 copy-start.7
  3.0 1.1 copy-start
  3.0 1.1 copy-start.1
  3.0 1.1 copy-start.2
  3.0 1.1 copy-start.3
  3.1 1.1 copy-start.4
  3.1 1.1 copy-start.5
  3.1 1.1 copy-start.6

commit v2 on v1

v2 whole, which is shorter than its diff:
```python
import functools

import jax
import jax.numpy as jnp
from jax import lax
from jax.experimental import pallas as pl
from jax.experimental.pallas import tpu as pltpu
from jax.sharding import PartitionSpec as P

LEVELS = 6
ROUNDS = 5
CAP = 16
BLOCKS = 48
GROUP = 8
UPW = 4
ZS, XS = 8, 4
PEERS = XS * ZS
OFFSETS = (0, -1, 1, -2, 2)
NEAR = len(OFFSETS)
ORDER = (2, 1, 3, 0)
ZERO = LEVELS * CAP
ARRIVED = ZERO + 1
STORE = ARRIVED + 2 * ROUNDS * PEERS
T_BLOCK, T_REF, T_SLOT, T_SEND, T_ROWS = 0, 1, 5, 8, 24
E_ROW1 = 2 * XS * NEAR
E_ROW2 = E_ROW1 + 4 * XS
ENTRIES = E_ROW2 + 2 * XS
MESH = pl.DeviceIdType.MESH
ROWS = 8
LANES = 128
PARTS = 4
WIDTH = LANES // PARTS
SLOTS = ROUNDS * PARTS


def groups_of(rows):
    return lax.broadcasted_iota(jnp.int32, (rows, LANES), 1) // WIDTH


def pick(group, values):
    result = values[PARTS - 1]
    for g in range(PARTS - 2, -1, -1):
        result = jnp.where(group == g, values[g], result)
    return result


def turns(value):
    return [value] + [pltpu.roll(value, WIDTH * t, 1) for t in range(1, PARTS)]


def make_table(z, level_ref, upwind_ref, send_in_ref, send_down_ref, table):
    square = (BLOCKS, BLOCKS)
    wide = (BLOCKS, LANES)
    row, col = (lax.broadcasted_iota(jnp.int32, square, d) for d in range(2))

    def down(mask, value):
        return jnp.sum(jnp.where(mask, value, 0), axis=0, keepdims=True)

    def upright(value):
        return jnp.sum(
            jnp.where(row == col, jnp.broadcast_to(value, square), 0), axis=1, keepdims=True
        )

    level = level_ref[...]
    level_col = upright(level)
    same = jnp.broadcast_to(level, square) == level_col
    rank_col = jnp.sum(jnp.where(same & (col < row), 1, 0), axis=1, keepdims=True)
    slot_col = level_col * CAP + rank_col
    table[...] = jnp.zeros(table.shape, jnp.int32)
    table[T_SLOT : T_SLOT + 1, :BLOCKS] = down(row == col, slot_col)
    here = slot_col == lax.broadcasted_iota(jnp.int32, wide, 1)
    table[T_BLOCK : T_BLOCK + 1, :] = down(here, lax.broadcasted_iota(jnp.int32, wide, 0))
    for j in range(UPW):
        t = upwind_ref[j : j + 1, :]
        local = ZERO + down(t == row, slot_col - ZERO)
        number = jnp.maximum(t - (BLOCKS + 1), 0)
        owner_z = number & (ZS - 1)
        away = (owner_z - z + ZS) & (ZS - 1)
        spot = jnp.zeros_like(away)
        for place, o in enumerate(OFFSETS + (3, 4, -3)):
            spot = jnp.where(away == o % ZS, place, spot)
        remote = ARRIVED + number - owner_z + spot
        ref = jnp.where(t <= BLOCKS, local, remote)
        table[T_REF + j : T_REF + j + 1, :] = ZERO + down(here, upright(ref) - ZERO)
    local_id = lax.broadcasted_iota(jnp.int32, (BLOCKS, PEERS), 0)
    for way, sent in enumerate((send_in_ref, send_down_ref)):
        for r in range(ROUNDS):
            place = T_SEND + way * ROUNDS + r
            table[place : place + 1, :PEERS] = CAP + down(sent[r] == local_id, rank_col - CAP)


def kernel(
    sections,
    level_ref,
    upwind_ref,
    send_in_ref,
    send_down_ref,
    residual,
    kin_ref,
    weight,
    frac,
    out,
    table,
    around,
    tab,
    tabs,
    kin,
    rights,
    factors,
    store,
    near,
    packs,
    arrived,
    sendb,
    pack_send,
    pack_recv,
    uni_send,
    uni_recv,
    tab_send,
    tab_recv,
    tab_local,
):
    sec = lax.axis_index("section")
    me = lax.axis_index("blk")
    x, z = me // ZS, lax.rem(me, ZS)
    has_next = sec < sections - 1
    has_prev = sec > 0
    columns = [lax.rem(x + xo, XS) * ZS for xo in range(XS)]
    rows = {zo: lax.rem(z + zo + ZS, ZS) for zo in range(-2, 3)}
    barrier = pltpu.get_barrier_semaphore()
    zeros = jnp.zeros((ROWS, LANES), jnp.float32)

    def at(section, xo, zo):
        return {"section": section, "blk": columns[xo] + rows[zo]}

    for xo in range(XS):
        for zo in range(-2, 3):
            if xo or zo:
                pl.semaphore_signal(
                    barrier, inc=1, device_id=at(sec, xo, zo), device_id_type=MESH
                )

    @pl.when(has_prev)
    def _():
        for xo in range(XS):
            for zo in range(-2, 3):
                pl.semaphore_signal(
                    barrier, inc=1, device_id=at(sec - 1, xo, zo), device_id_type=MESH
                )

    group = groups_of(ROWS)

    def prepare(b, _):
        exact = kin_ref[b]
        coarse = exact.astype(jnp.bfloat16).astype(jnp.float32)
        kin[b] = jnp.concatenate([coarse, exact - coarse, coarse], axis=1).astype(jnp.bfloat16)
        whole = residual[b]
        turned = [turns(whole[g * ROWS : (g + 1) * ROWS]) for g in range(PARTS)]
        scales = turns(jnp.concatenate([frac[b], weight[b], weight[b], frac[b][:2]], axis=0))
        for part in range(PARTS):
            rights[part, b] = pick(
                group, [turned[g][(g - part) % PARTS] for g in range(PARTS)]
            )
            factors[part, b] = pick(
                group, [scales[(g - part) % PARTS] for g in range(PARTS)]
            )
        return 0

    def solve(part, level, slot, last=False):
        def gather(k):
            place = level * CAP + k
            b = tab[T_BLOCK, place]
            inflow = rights[part, b]
            factor = factors[part, b]
            for j in range(UPW):
                source = store[part, tab[T_REF + j, place]]
                inflow = inflow + factor[j : j + 1, :] * source
            turned = turns(inflow)
            all_species = jnp.concatenate(
                [
                    pick(group, [turned[(to - g) % PARTS] for to in range(PARTS)])
                    for g in range(PARTS)
                ],
                axis=0,
            )
            coarse = all_species.astype(jnp.bfloat16)
            rest = (all_species - coarse.astype(jnp.float32)).astype(jnp.bfloat16)
            return b, factor[UPW : UPW + 1, :], jnp.concatenate([coarse, coarse, rest], axis=0)

        def batch(i, _):
            spots = [i * GROUP + k for k in range(GROUP)]
            gathered = [gather(k) for k in spots]
            mixed = [
                jnp.dot(kin[b], terms, preferred_element_type=jnp.float32)
                for b, _, terms in gathered
            ]
            solved = [
                scale * pick(group, [m[g * ROWS : (g + 1) * ROWS] for g in range(PARTS)])
                for (_, scale, _), m in zip(gathered, mixed)
            ]
            for k, value in zip(spots, solved):
                store[part, level * CAP + k] = value
                if not last:
                    packs[slot, k] = value
                    near[part, k] = value
            return 0

        lax.fori_loop(0, CAP // GROUP, batch, 0)

    def pack_copy(slot, source, target, zo):
        return pltpu.make_async_remote_copy(
            src_ref=packs.at[slot, pl.ds(source * CAP, CAP)],
            dst_ref=packs.at[slot, pl.ds(target * CAP, CAP)],
            send_sem=pack_send.at[slot],
            recv_sem=pack_recv.at[slot, target],
            device_id=at(sec, 0, zo),
            device_id_type=MESH,
        )

    def pack_wait(slot, p):
        some = packs.at[slot, pl.ds(p * CAP, CAP)]
        pltpu.make_async_copy(some, some, pack_recv.at[slot, p]).wait()

    def hold(slot, p):
        part = lax.rem(slot, PARTS)
        for k in range(CAP):
            near[part, p * (CAP + 1) + k] = packs[slot, p * CAP + k]

    def fill(slot, entry, way, p, xo, zo):
        level, part = slot // PARTS, lax.rem(slot, PARTS)
        chosen = tabs[p, way * ROUNDS + level, columns[xo] + rows[zo]]
        sendb[slot, entry] = near[part, p * (CAP + 1) + chosen]

    def copy(slot, entry, count, way, place, xo, zo):
        return pltpu.make_async_remote_copy(
            src_ref=sendb.at[slot, pl.ds(entry, count)],
            dst_ref=arrived.at[way, slot, pl.ds(x * ZS + place, count)],
            send_sem=uni_send.at[way, slot],
            recv_sem=uni_recv.at[way, slot],
            device_id=at(sec + way, xo, zo),
            device_id_type=MESH,
        )

    def to_row(slot, way, xo, first, count):
        entry = (way * XS + xo) * NEAR
        for p in range(first, first + count):
            fill(slot, entry + p, way, p, xo, 0)
        if way or xo:
            copy(slot, entry + first, count, way, first, xo, 0).start()

    def to_columns(send_way):
        for xo in ORDER:
            send_way(xo, 0)

        @pl.when(has_next)
        def _():
            for xo in ORDER:
                send_way(xo, 1)

    def send_own(slot):
        pack_copy(slot, 0, 1, 1).start()
        pack_copy(slot, 0, 2, -1).start()

    def forward(slot):
        pack_wait(slot, 1)
        pack_copy(slot, 1, 3, 1).start()
        pack_wait(slot, 2)
        pack_copy(slot, 2, 4, -1).start()
        hold(slot, 1)
        hold(slot, 2)
        to_columns(lambda xo, way: to_row(slot, way, xo, 0, 3))

    def deliver(slot):
        for p in (3, 4):
            pack_wait(slot, p)
            hold(slot, p)

        def send_way(xo, way):
            far = E_ROW2 + way * XS + xo
            p, zo = ((3, 2), (4, -2))[way]
            fill(slot, far, way, p, xo, zo)
            copy(slot, far, 1, way, 6, xo, zo).start()
            up = E_ROW1 + way * XS + xo
            fill(slot, up, way, 3, xo, 1)
            copy(slot, up, 1, way, 7, xo, 1).start()
            down = E_ROW1 + (2 + way) * XS + xo
            fill(slot, down, way, 4, xo, -1)
            copy(slot, down, 1, way, 5, xo, -1).start()
            to_row(slot, way, xo, 3, 2)

        to_columns(send_way)

    def absorb(slot):
        level, part = slot // PARTS, lax.rem(slot, PARTS)
        some = arrived.at[0, slot, pl.ds(0, PEERS - NEAR)]
        pltpu.make_async_copy(some, some, uni_recv.at[0, slot]).wait()
        base = ARRIVED + level * PEERS
        for i in range(PEERS):
            store[part, base + i] = arrived[0, slot, i]
        for p in range(NEAR):
            store[part, base + x * ZS + p] = sendb[slot, p]

        @pl.when(has_prev)
        def _():
            every = arrived.at[1, slot]
            pltpu.make_async_copy(every, every, uni_recv.at[1, slot]).wait()
            for i in range(PEERS):
                store[part, base + ROUNDS * PEERS + i] = arrived[1, slot, i]

    make_table(z, level_ref, upwind_ref, send_in_ref, send_down_ref, table)
    moves = [
        pltpu.make_async_copy(table, tab, tab_local.at[NEAR]),
        pltpu.make_async_copy(table.at[pl.ds(T_SEND, 16)], tabs.at[0], tab_local.at[0]),
    ]
    for move in moves:
        move.start()
    lax.fori_loop(0, BLOCKS, prepare, 0, unroll=8)
    for part in range(PARTS):
        store[part, ZERO] = zeros
        for p in range(NEAR):
            near[part, p * (CAP + 1) + CAP] = zeros

    @pl.when(jnp.logical_not(has_prev))
    def _():
        def blank(i, _):
            for part in range(PARTS):
                store[part, ARRIVED + ROUNDS * PEERS + i] = zeros
            return 0

        lax.fori_loop(0, ROUNDS * PEERS, blank, 0)

    for move in moves:
        move.wait()
    solve(0, 0, 0)

    @pl.when(has_next)
    def _():
        pl.semaphore_wait(barrier, 2 * XS * NEAR - 1)

    @pl.when(jnp.logical_not(has_next))
    def _():
        pl.semaphore_wait(barrier, XS * NEAR - 1)

    send_own(0)
    for o in OFFSETS[1:]:
        p = OFFSETS.index(-o)
        pltpu.make_async_remote_copy(
            src_ref=table.at[pl.ds(T_SEND, 16)],
            dst_ref=around.at[p],
            send_sem=tab_send,
            recv_sem=tab_recv.at[p],
            device_id=at(sec, 0, o),
            device_id_type=MESH,
        ).start()

    def first(part, _):
        solve(part, 0, part)
        send_own(part)
        return 0

    lax.fori_loop(1, PARTS, first, 0)
    moves = []
    for p in range(1, NEAR):
        source = around.at[p]
        pltpu.make_async_copy(source, source, tab_recv.at[p]).wait()
        moves.append(pltpu.make_async_copy(source, tabs.at[p], tab_local.at[p]))
        moves[-1].start()
    for move in moves:
        move.wait()
    forward(0)

    def step(slot, _):
        @pl.when(slot >= PARTS)
        def _():
            absorb(slot - PARTS)
            solve(lax.rem(slot, PARTS), slot // PARTS, slot)
            send_own(slot)

        forward(slot - 1)
        deliver(slot - 2)
        return 0

    lax.fori_loop(2, SLOTS, step, 0)
    absorb(SLOTS - PARTS)
    solve(0, ROUNDS, 0, last=True)
    forward(SLOTS - 1)
    deliver(SLOTS - 2)
    absorb(SLOTS - PARTS + 1)
    solve(1, ROUNDS, 0, last=True)
    deliver(SLOTS - 1)

    def tail(part, _):
        absorb(SLOTS - PARTS + part)
        solve(part, ROUNDS, 0, last=True)
        return 0

    lax.fori_loop(2, PARTS, tail, 0)

    def give(b, _):
        place = tab[T_SLOT, b]
        turned = [turns(store[part, place]) for part in range(PARTS)]
        for g in range(PARTS):
            out[b, g * ROWS : (g + 1) * ROWS] = pick(
                group, [turned[part][(part - g) % PARTS] for part in range(PARTS)]
            )
        return 0

    lax.fori_loop(0, BLOCKS, give, 0, unroll=4)

    def finish(slot, _):
        some = packs.at[slot, pl.ds(0, 4 * CAP)]
        pltpu.make_async_copy(some, some, pack_send.at[slot]).wait()
        some = sendb.at[slot, pl.ds(0, PEERS - NEAR)]
        pltpu.make_async_copy(some, some, uni_send.at[0, slot]).wait()

        @pl.when(has_next)
        def _():
            some = sendb.at[slot, pl.ds(0, PEERS)]
            pltpu.make_async_copy(some, some, uni_send.at[1, slot]).wait()

        return 0

    lax.fori_loop(0, SLOTS, finish, 0)
    some = around.at[pl.ds(0, NEAR - 1)]
    pltpu.make_async_copy(some, some, tab_send).wait()


def shards(
    residual, kin_inverse, cell_weight, upwind_frac, block_level, send_in, send_down, upwind_slot
):
    blocks, species, cells = residual.shape
    vmem = pl.BlockSpec(memory_space=pltpu.VMEM)
    piece = (ROWS, LANES)
    return pl.pallas_call(
        functools.partial(kernel, lax.axis_size("section")),
        out_shape=jax.ShapeDtypeStruct(residual.shape, jnp.float32),
        in_specs=[vmem] * 8,
        out_specs=vmem,
        scratch_shapes=[
            pltpu.VMEM((T_ROWS, LANES), jnp.int32),
            pltpu.VMEM((NEAR, 16, LANES), jnp.int32),
            pltpu.SMEM((T_ROWS, LANES), jnp.int32),
            pltpu.SMEM((NEAR, 16, LANES), jnp.int32),
            pltpu.VMEM((blocks, species, 3 * species), jnp.bfloat16),
            pltpu.VMEM((PARTS, BLOCKS, *piece), jnp.float32),
            pltpu.VMEM((PARTS, BLOCKS, *piece), jnp.float32),
            pltpu.VMEM((PARTS, STORE, *piece), jnp.float32),
            pltpu.VMEM((PARTS, NEAR * (CAP + 1), *piece), jnp.float32),
            pltpu.VMEM((SLOTS, NEAR * CAP, *piece), jnp.float32),
            pltpu.VMEM((2, SLOTS, PEERS, *piece), jnp.float32),
            pltpu.VMEM((SLOTS, ENTRIES, *piece), jnp.float32),
            pltpu.SemaphoreType.DMA((SLOTS,)),
            pltpu.SemaphoreType.DMA((SLOTS, NEAR)),
            pltpu.SemaphoreType.DMA((2, SLOTS)),
            pltpu.SemaphoreType.DMA((2, SLOTS)),
            pltpu.SemaphoreType.DMA,
            pltpu.SemaphoreType.DMA((NEAR,)),
            pltpu.SemaphoreType.DMA((NEAR + 1,)),
        ],
        compiler_params=pltpu.CompilerParams(
            collective_id=0, has_side_effects=True, vmem_limit_bytes=44 * 1024 * 1024
        ),
    )(
        block_level[None],
        upwind_slot.T,
        send_in.transpose(1, 0, 2),
        send_down.transpose(1, 0, 2),
        residual,
        kin_inverse,
        cell_weight[:, None, :],
        upwind_frac,
    )


def solution(mesh):
    both = ("section", "blk")
    return jax.shard_map(
        shards,
        mesh=mesh,
        in_specs=(
            P(both, None, None),
            P(both, None, None),
            P(both, None),
            P(both, None, None),
            P(both),
            P(both, None, None),
            P(both, None, None),
            P(both, None),
        ),
        out_specs=P(both, None, None),
        check_vma=False,
    )
```

time: 131 us -> 114 us (0.87)
  the two profiles are of different devices: /device:TPU:41 before, /device:TPU:17 now
where the time goes in v2:
time: 114 us
  Pallas kernels  111 us (97%)
  local copies, waits for them, and re-layouts  2.72 us (2%)
    pallas_call x1, Pallas kernels, shards(): pl.pallas_call(functools.partial(kernel, lax.axis_size('section')), out_s...  111 us
    unnamed x16, local copies, waits for them, and re-layouts  2.72 us

profile of v2, /device:TPU:17, one launch (start us, length us, event | category | flops | bytes accessed | tf_op | source)
XLA Modules:
  0.0 113.8 jit_solution(4725100590500993920)
XLA Ops:
  0.0 0.0 copy-start
  0.0 0.0 copy-start.1
  0.0 0.0 copy-start.2
  0.0 0.0 copy-start.3
  0.0 0.0 copy-start.4
  0.0 0.0 copy-start.5
  0.0 0.0 copy-start.6
  0.0 1.8 %copy.9.kin_ref = f32[48,32,32]{2,1,0:T(8,128)S(1)} copy(f32[48,32,32]{0,2,1:T(8,128)} %param.9) | data formatting | bytes 393216 | tf_op args[1]
  1.9 0.0 copy-done
  1.9 0.0 copy-done.1
  1.9 0.0 copy-done.2
  1.9 0.0 copy-done.3
  1.9 0.0 copy-done.4
  1.9 0.0 copy-done.5
  1.9 0.0 copy-done.6
  1.9 111.0 %shard_map.82 = f32[48,32,128]{2,1,0:T(8,128)S(1)} custom-call(s32[1,48]{1,0:T(1,128)S(1)} %bitcast.9, s32[4,48]{1,0:T(4,128)S(1)} %bitcast.8, s32[5,1,32]{2,1,0:T(1,128)S(1)} %bitcast.6, s32[5,1,32]{2,1,0:T(1,128)S(1)} %bitcast.7, f32[48,32,128]{2,1,0:T(8,128)S(1)} %copy-done, f32[48,32,32]{2,1,0:T(8,128)S(1)} %copy.9.kin_ref, f32[48,1,128]{2,1,0:T(1,128)S(1)} %bitcast.5, ...), custom_call_target="tpu_custom_call" | custom-call | tf_op jit(solution)/shard_map/pallas_call | solution.py:434
  112.9 0.9 copy.11
Async XLA Ops:
  0.0 1.9 %copy-start = (f32[48,32,128]{2,1,0:T(8,128)S(1)}, f32[48,32,128]{2,1,0:T(8,128)}, u32[]{:S(2)}) copy-start(f32[48,32,128]{2,1,0:T(8,128)} %residual.1) | copy-start | bytes 2359300
  0.0 1.9 %copy-start.1 = (f32[48,4,128]{2,1,0:T(4,128)S(1)}, f32[48,4,128]{2,1,0:T(4,128)}, u32[]{:S(2)}) copy-start(f32[48,4,128]{2,1,0:T(4,128)} %frac.1) | copy-start | bytes 294916
  0.0 1.9 %copy-start.2 = (f32[48,128]{1,0:T(8,128)S(1)}, f32[48,128]{1,0:T(8,128)}, u32[]{:S(2)}) copy-start(f32[48,128]{1,0:T(8,128)} %param.10) | copy-start | bytes 73732
  0.0 1.9 %copy-start.3 = (s32[1,5,32]{2,0,1:T(1,128)S(1)}, s32[1,5,32]{2,0,1:T(1,128)}, u32[]{:S(2)}) copy-start(s32[1,5,32]{2,0,1:T(1,128)} %param.13) | copy-start | bytes 1924
  0.0 1.9 %copy-start.4 = (s32[1,5,32]{2,0,1:T(1,128)S(1)}, s32[1,5,32]{2,0,1:T(1,128)}, u32[]{:S(2)}) copy-start(s32[1,5,32]{2,0,1:T(1,128)} %param.14) | copy-start | bytes 1924
  0.0 1.9 %copy-start.5 = (s32[48,4]{0,1:T(4,128)S(1)}, s32[48,4]{0,1:T(4,128)}, u32[]{:S(2)}) copy-start(s32[48,4]{0,1:T(4,128)} %param.15) | copy-start | bytes 2308
  0.0 1.9 %copy-start.6 = (s32[48]{0:T(128)S(1)}, s32[48]{0:T(128)}, u32[]{:S(2)}) copy-start(s32[48]{0:T(128)} %param.12) | copy-start | bytes 580

commit v3 on v2

--- a/solution.py
+++ b/solution.py
@@ -11,7 +11,7 @@
 ROUNDS = 5
 CAP = 16
 BLOCKS = 48
-GROUP = 8
+GROUP = 16
 UPW = 4
 ZS, XS = 8, 4
 PEERS = XS * ZS
@@ -31,6 +31,7 @@
 PARTS = 4
 WIDTH = LANES // PARTS
 SLOTS = ROUNDS * PARTS
+LAG = 6
 
 
 def groups_of(rows):
@@ -150,20 +151,27 @@
 
     group = groups_of(ROWS)
 
-    def prepare(b, _):
-        exact = kin_ref[b]
-        coarse = exact.astype(jnp.bfloat16).astype(jnp.float32)
-        kin[b] = jnp.concatenate([coarse, exact - coarse, coarse], axis=1).astype(jnp.bfloat16)
+    def prepare(parts, b):
         whole = residual[b]
         turned = [turns(whole[g * ROWS : (g + 1) * ROWS]) for g in range(PARTS)]
         scales = turns(jnp.concatenate([frac[b], weight[b], weight[b], frac[b][:2]], axis=0))
-        for part in range(PARTS):
+        for part in parts:
             rights[part, b] = pick(
                 group, [turned[g][(g - part) % PARTS] for g in range(PARTS)]
             )
             factors[part, b] = pick(
                 group, [scales[(g - part) % PARTS] for g in range(PARTS)]
             )
+
+    def prepare_first(b, _):
+        exact = kin_ref[b]
+        coarse = exact.astype(jnp.bfloat16).astype(jnp.float32)
+        kin[b] = jnp.concatenate([coarse, exact - coarse, coarse], axis=1).astype(jnp.bfloat16)
+        prepare((0,), b)
+        return 0
+
+    def prepare_rest(b, _):
+        prepare(range(1, PARTS), b)
         return 0
 
     def solve(part, level, slot, last=False):
@@ -314,7 +322,7 @@
     ]
     for move in moves:
         move.start()
-    lax.fori_loop(0, BLOCKS, prepare, 0, unroll=8)
+    lax.fori_loop(0, BLOCKS, prepare_first, 0, unroll=8)
     for part in range(PARTS):
         store[part, ZERO] = zeros
         for p in range(NEAR):
@@ -352,6 +360,7 @@
             device_id=at(sec, 0, o),
             device_id_type=MESH,
         ).start()
+    lax.fori_loop(0, BLOCKS, prepare_rest, 0, unroll=8)
 
     def first(part, _):
         solve(part, 0, part)
@@ -369,6 +378,19 @@
         move.wait()
     forward(0)
 
+    def finish(slot, _):
+        some = packs.at[slot, pl.ds(0, 4 * CAP)]
+        pltpu.make_async_copy(some, some, pack_send.at[slot]).wait()
+        some = sendb.at[slot, pl.ds(0, PEERS - NEAR)]
+        pltpu.make_async_copy(some, some, uni_send.at[0, slot]).wait()
+
+        @pl.when(has_next)
+        def _():
+            some = sendb.at[slot, pl.ds(0, PEERS)]
+            pltpu.make_async_copy(some, some, uni_send.at[1, slot]).wait()
+
+        return 0
+
     def step(slot, _):
         @pl.when(slot >= PARTS)
         def _():
@@ -378,6 +400,11 @@
 
         forward(slot - 1)
         deliver(slot - 2)
+
+        @pl.when(slot >= LAG)
+        def _():
+            finish(slot - LAG, 0)
+
         return 0
 
     lax.fori_loop(2, SLOTS, step, 0)
@@ -405,22 +432,9 @@
             )
         return 0
 
-    lax.fori_loop(0, BLOCKS, give, 0, unroll=4)
-
-    def finish(slot, _):
-        some = packs.at[slot, pl.ds(0, 4 * CAP)]
-        pltpu.make_async_copy(some, some, pack_send.at[slot]).wait()
-        some = sendb.at[slot, pl.ds(0, PEERS - NEAR)]
-        pltpu.make_async_copy(some, some, uni_send.at[0, slot]).wait()
-
-        @pl.when(has_next)
-        def _():
-            some = sendb.at[slot, pl.ds(0, PEERS)]
-            pltpu.make_async_copy(some, some, uni_send.at[1, slot]).wait()
-
-        return 0
-
-    lax.fori_loop(0, SLOTS, finish, 0)
+    lax.fori_loop(0, BLOCKS, give, 0, unroll=8)
+
+    lax.fori_loop(SLOTS - LAG, SLOTS, finish, 0)
     some = around.at[pl.ds(0, NEAR - 1)]
     pltpu.make_async_copy(some, some, tab_send).wait()
 

time: 114 us -> 112 us (0.982)
  the two profiles are of different devices: /device:TPU:17 before, /device:TPU:9 now
where the time goes in v3:
time: 112 us
  Pallas kernels  109 us (97%)
  local copies, waits for them, and re-layouts  2.72 us (2%)
    pallas_call x1, Pallas kernels, shards(): pl.pallas_call(functools.partial(kernel, lax.axis_size('section')), out_s...  109 us
    unnamed x16, local copies, waits for them, and re-layouts  2.72 us

profile of v3, /device:TPU:9, one launch (start us, length us, event | category | flops | bytes accessed | tf_op | source)
XLA Modules:
  0.0 112.3 jit_solution(7164929716249830394)
XLA Ops:
  0.0 0.0 copy-start
  0.0 0.0 copy-start.1
  0.0 0.0 copy-start.2
  0.0 0.0 copy-start.3
  0.0 0.0 copy-start.4
  0.0 0.0 copy-start.5
  0.0 0.0 copy-start.6
  0.0 1.8 %copy.9.kin_ref = f32[48,32,32]{2,1,0:T(8,128)S(1)} copy(f32[48,32,32]{0,2,1:T(8,128)} %param.9) | data formatting | bytes 393216 | tf_op args[1]
  1.9 0.0 copy-done
  1.9 0.0 copy-done.1
  1.9 0.0 copy-done.2
  1.9 0.0 copy-done.3
  1.9 0.0 copy-done.4
  1.9 0.0 copy-done.5
  1.9 0.0 copy-done.6
  1.9 109.5 %shard_map.82 = f32[48,32,128]{2,1,0:T(8,128)S(1)} custom-call(s32[1,48]{1,0:T(1,128)S(1)} %bitcast.9, s32[4,48]{1,0:T(4,128)S(1)} %bitcast.8, s32[5,1,32]{2,1,0:T(1,128)S(1)} %bitcast.6, s32[5,1,32]{2,1,0:T(1,128)S(1)} %bitcast.7, f32[48,32,128]{2,1,0:T(8,128)S(1)} %copy-done, f32[48,32,32]{2,1,0:T(8,128)S(1)} %copy.9.kin_ref, f32[48,1,128]{2,1,0:T(1,128)S(1)} %bitcast.5, ...), custom_call_target="tpu_custom_call" | custom-call | tf_op jit(solution)/shard_map/pallas_call | solution.py:448
  111.4 0.9 copy.11
Async XLA Ops:
  0.0 1.9 %copy-start = (f32[48,32,128]{2,1,0:T(8,128)S(1)}, f32[48,32,128]{2,1,0:T(8,128)}, u32[]{:S(2)}) copy-start(f32[48,32,128]{2,1,0:T(8,128)} %residual.1) | copy-start | bytes 2359300
  0.0 1.9 %copy-start.1 = (f32[48,4,128]{2,1,0:T(4,128)S(1)}, f32[48,4,128]{2,1,0:T(4,128)}, u32[]{:S(2)}) copy-start(f32[48,4,128]{2,1,0:T(4,128)} %frac.1) | copy-start | bytes 294916
  0.0 1.9 %copy-start.2 = (f32[48,128]{1,0:T(8,128)S(1)}, f32[48,128]{1,0:T(8,128)}, u32[]{:S(2)}) copy-start(f32[48,128]{1,0:T(8,128)} %param.10) | copy-start | bytes 73732
  0.0 1.9 %copy-start.3 = (s32[1,5,32]{2,0,1:T(1,128)S(1)}, s32[1,5,32]{2,0,1:T(1,128)}, u32[]{:S(2)}) copy-start(s32[1,5,32]{2,0,1:T(1,128)} %param.13) | copy-start | bytes 1924
  0.0 1.9 %copy-start.4 = (s32[1,5,32]{2,0,1:T(1,128)S(1)}, s32[1,5,32]{2,0,1:T(1,128)}, u32[]{:S(2)}) copy-start(s32[1,5,32]{2,0,1:T(1,128)} %param.14) | copy-start | bytes 1924
  0.0 1.9 %copy-start.5 = (s32[48,4]{0,1:T(4,128)S(1)}, s32[48,4]{0,1:T(4,128)}, u32[]{:S(2)}) copy-start(s32[48,4]{0,1:T(4,128)} %param.15) | copy-start | bytes 2308
  0.0 1.9 %copy-start.6 = (s32[48]{0:T(128)S(1)}, s32[48]{0:T(128)}, u32[]{:S(2)}) copy-start(s32[48]{0:T(128)} %param.12) | copy-start | bytes 580

commit v4 on v3

--- a/solution.py
+++ b/solution.py
@@ -274,6 +274,8 @@
         pack_copy(slot, 1, 3, 1).start()
         pack_wait(slot, 2)
         pack_copy(slot, 2, 4, -1).start()
+
+    def spread(slot):
         hold(slot, 1)
         hold(slot, 2)
         to_columns(lambda xo, way: to_row(slot, way, xo, 0, 3))
@@ -377,6 +379,7 @@
     for move in moves:
         move.wait()
     forward(0)
+    spread(0)
 
     def finish(slot, _):
         some = packs.at[slot, pl.ds(0, 4 * CAP)]
@@ -400,6 +403,7 @@
 
         forward(slot - 1)
         deliver(slot - 2)
+        spread(slot - 1)
 
         @pl.when(slot >= LAG)
         def _():
@@ -412,6 +416,7 @@
     solve(0, ROUNDS, 0, last=True)
     forward(SLOTS - 1)
     deliver(SLOTS - 2)
+    spread(SLOTS - 1)
     absorb(SLOTS - PARTS + 1)
     solve(1, ROUNDS, 0, last=True)
     deliver(SLOTS - 1)

time: 112 us -> 113 us (level)
  the two profiles are of different devices: /device:TPU:9 before, /device:TPU:17 now
where the time goes in v4:
time: 113 us
  Pallas kernels  110 us (97%)
  local copies, waits for them, and re-layouts  2.72 us (2%)
    pallas_call x1, Pallas kernels, shards(): pl.pallas_call(functools.partial(kernel, lax.axis_size('section')), out_s...  110 us
    unnamed x16, local copies, waits for them, and re-layouts  2.72 us

profile of v4, /device:TPU:17, one launch (start us, length us, event | category | flops | bytes accessed | tf_op | source)
XLA Modules:
  0.0 112.6 jit_solution(14998363281303327154)
XLA Ops:
  0.0 0.0 copy-start
  0.0 0.0 copy-start.1
  0.0 0.0 copy-start.2
  0.0 0.0 copy-start.3
  0.0 0.0 copy-start.4
  0.0 0.0 copy-start.5
  0.0 0.0 copy-start.6
  0.0 1.8 %copy.9.kin_ref = f32[48,32,32]{2,1,0:T(8,128)S(1)} copy(f32[48,32,32]{0,2,1:T(8,128)} %param.9) | data formatting | bytes 393216 | tf_op args[1]
  1.9 0.0 copy-done
  1.9 0.0 copy-done.1
  1.9 0.0 copy-done.2
  1.9 0.0 copy-done.3
  1.9 0.0 copy-done.4
  1.9 0.0 copy-done.5
  1.9 0.0 copy-done.6
  1.9 109.7 %shard_map.82 = f32[48,32,128]{2,1,0:T(8,128)S(1)} custom-call(s32[1,48]{1,0:T(1,128)S(1)} %bitcast.9, s32[4,48]{1,0:T(4,128)S(1)} %bitcast.8, s32[5,1,32]{2,1,0:T(1,128)S(1)} %bitcast.6, s32[5,1,32]{2,1,0:T(1,128)S(1)} %bitcast.7, f32[48,32,128]{2,1,0:T(8,128)S(1)} %copy-done, f32[48,32,32]{2,1,0:T(8,128)S(1)} %copy.9.kin_ref, f32[48,1,128]{2,1,0:T(1,128)S(1)} %bitcast.5, ...), custom_call_target="tpu_custom_call" | custom-call | tf_op jit(solution)/shard_map/pallas_call | solution.py:453
  111.7 0.9 copy.11
Async XLA Ops:
  0.0 1.9 %copy-start = (f32[48,32,128]{2,1,0:T(8,128)S(1)}, f32[48,32,128]{2,1,0:T(8,128)}, u32[]{:S(2)}) copy-start(f32[48,32,128]{2,1,0:T(8,128)} %residual.1) | copy-start | bytes 2359300
  0.0 1.9 %copy-start.1 = (f32[48,4,128]{2,1,0:T(4,128)S(1)}, f32[48,4,128]{2,1,0:T(4,128)}, u32[]{:S(2)}) copy-start(f32[48,4,128]{2,1,0:T(4,128)} %frac.1) | copy-start | bytes 294916
  0.0 1.9 %copy-start.2 = (f32[48,128]{1,0:T(8,128)S(1)}, f32[48,128]{1,0:T(8,128)}, u32[]{:S(2)}) copy-start(f32[48,128]{1,0:T(8,128)} %param.10) | copy-start | bytes 73732
  0.0 1.9 %copy-start.3 = (s32[1,5,32]{2,0,1:T(1,128)S(1)}, s32[1,5,32]{2,0,1:T(1,128)}, u32[]{:S(2)}) copy-start(s32[1,5,32]{2,0,1:T(1,128)} %param.13) | copy-start | bytes 1924
  0.0 1.9 %copy-start.4 = (s32[1,5,32]{2,0,1:T(1,128)S(1)}, s32[1,5,32]{2,0,1:T(1,128)}, u32[]{:S(2)}) copy-start(s32[1,5,32]{2,0,1:T(1,128)} %param.14) | copy-start | bytes 1924
  0.0 1.9 %copy-start.5 = (s32[48,4]{0,1:T(4,128)S(1)}, s32[48,4]{0,1:T(4,128)}, u32[]{:S(2)}) copy-start(s32[48,4]{0,1:T(4,128)} %param.15) | copy-start | bytes 2308
  0.0 1.9 %copy-start.6 = (s32[48]{0:T(128)S(1)}, s32[48]{0:T(128)}, u32[]{:S(2)}) copy-start(s32[48]{0:T(128)} %param.12) | copy-start | bytes 580
